TPU v7x, 32 devices: a whole 2x2x4 slice. The times are simulated.
32 devices in a mesh: pipe: 2 (over x), dp: 4 (over z), tensor: 4 (over y, core).
Axes of the slice: x: 2, y: 2, z: 4, core: 2. Of those that a mesh axis runs over, the one named last changes fastest.
Arguments:
- section_input: bfloat16 [2, 24, 512, 768], P('pipe', 'dp', 'tensor'), may hold values from -6 to 6
- lengths: int32 [24, 2], P('dp'), may hold values from 32 to 512, as said below
- norm_gain: float32 [2, 3, 768], P('pipe'), may hold values from 0.5 to 1.5
- attn_in: bfloat16 [2, 3, 768, 768], P('pipe', None, None, 'tensor'), may hold values from -0.21875 to 0.21875
- attn_out: bfloat16 [2, 768, 768], P('pipe', 'tensor'), may hold values from -2.5 to 2.5
- cross_first: bfloat16 [2, 768, 768], P('pipe', None, 'tensor'), may hold values from -0.21875 to 0.21875
- cross_second: bfloat16 [2, 768, 768], P('pipe', None, 'tensor')
- ffn_in: bfloat16 [2, 768, 3072], P('pipe', None, 'tensor'), may hold values from -0.21875 to 0.21875
- ffn_out: bfloat16 [2, 3072, 768], P('pipe', 'tensor'), may hold values from -0.109375 to 0.109375
- rel_bias: bfloat16 [2, 32, 12], P('pipe', None, 'tensor'), may hold values from -4 to 4
- out_grad: bfloat16 [2, 24, 512, 768], P('pipe', 'dp', 'tensor'), may hold values from -6 to 6
Outputs:
- section_output: bfloat16 [2, 24, 512, 768], P('pipe', 'dp', 'tensor')
- input_grad: float32 [2, 24, 512, 768], P('pipe', 'dp', 'tensor')
- attn_in_grad: float32 [2, 3, 768, 768], P('pipe', None, 'dp', 'tensor')
- attn_out_grad: float32 [2, 768, 768], P('pipe', 'tensor', 'dp')
- cross_first_grad: float32 [2, 768, 768], P('pipe', 'dp', 'tensor')
- cross_second_grad: float32 [2, 768, 768], P('pipe', 'dp', 'tensor')
- ffn_in_grad: float32 [2, 768, 3072], P('pipe', 'dp', 'tensor')
- ffn_out_grad: float32 [2, 3072, 768], P('pipe', 'tensor', 'dp')
- rel_bias_grad: float32 [2, 32, 12], P('pipe', 'dp', 'tensor')
- norm_gain_grad: float32 [2, 3, 768], P('pipe', None, ('dp', 'tensor'))
Inputs may be any that keep to these rules, and one draw needn't show every extreme that they name: `lengths`: in each block of 6 rows (one data index) one row, drawn from the seed, has length 512 in both columns.
All inputs are finite; a program needn't handle non-finite values.
Results may differ from a plain program's by a relative error of at most 0.03.
Values may be sent and summed in bfloat16 or wider, within the bound.
A program may use at most 320 MiB of HBM per device.

v0:
```python
import math
from functools import partial

import jax
import jax.numpy as jnp
import numpy as np
from jax import lax
from jax.experimental import pallas as pl
from jax.experimental.pallas import tpu as pltpu
from jax.sharding import PartitionSpec as P

NB = 32
MAX_DIST = 128
DK = 64
EPS = 1e-06
MASKED = -1000000000.0
MESH = pl.DeviceIdType.MESH
bf16, f32 = jnp.bfloat16, jnp.float32
PAIR = 128
G_IN, G_MID, G_FFN, G_DFFN, G_DMID, G_DATT = range(6)
S_ATT, S_MID, S_FFN, S_DMEM, S_DFFN, S_DMID, S_DIN = range(7)


def bucket_list(offsets, both_ways):
    half = NB // 2 if both_ways else NB
    exact = half // 2
    out = []
    for r in offsets:
        base = half if both_ways and r > 0 else 0
        n = abs(r) if both_ways else max(-r, 0)
        if n < exact:
            out.append(base + n)
        else:
            at = exact + math.floor(
                math.log(n / exact) / math.log(MAX_DIST / exact) * (half - exact)
            )
            out.append(base + min(half - 1, at))
    return out


def nt(a, b):
    return lax.dot_general(a, b, (((1,), (1,)), ((), ())), preferred_element_type=f32)


def nn(a, b):
    return lax.dot_general(a, b, (((1,), (0,)), ((), ())), preferred_element_type=f32)


def tn(a, b):
    return lax.dot_general(a, b, (((0,), (0,)), ((), ())), preferred_element_type=f32)


W_Q, W_K, W_V, W_O, W_C1, W_C2 = range(6)
W_F1, W_F2, WEIGHTS = range(6, 10), range(10, 14), 14


def section_kernel(
    xin, cin, w_in, w_out, c_1, c_2, f_1, f_2, gain_ref, len_ref, table_ref, hot_ref,
    sec_out, ing_out, zs, zr, fin_out, small_out, gown, ysend, yrecv,
    wqkv, wo, w1, w2, wf1, wf2, bias,
    xr, cot, out_rows,
    fin, qkv, ctx, lse, h1, fatt, mid, kvs, kvr,
    r2, ffnf, fffn, dctx, rsa, rss, rsr, diag, small, small_c, small_y, small_z,
    lsem, xs, xg, ts, tg, ys, yg, zps, zpg, gs, gr, ss, sr, ps, pr, os, og, us, ug, vs, vg, ms, mg,
    *, direct,
):
    ex, _, tb, width = xr.shape
    fmid = fatt
    rows = 2 * tb
    kq = wo.shape[0] // 2
    kc = wo.shape[0]
    fq = wf1.shape[2]
    fc = 2 * fq
    seq = 2 * rows
    heads = kc // DK
    pairs = kc // PAIR
    own_heads = heads // 2

    tensor = lax.axis_index("tensor")
    pipe = lax.axis_index("pipe")
    data = lax.axis_index("dp")
    count = lax.axis_size("dp")
    core = lax.rem(tensor, 2)
    side = tensor // 2
    parity = lax.rem(data, 2)
    partner = {"tensor": tensor + 1 - 2 * core}
    peer = {"tensor": lax.rem(tensor + 2, 4)}
    near = {"dp": data + 1 - 2 * parity}
    other = {"pipe": 1 - pipe}

    def away(step):
        return lax.rem(data + step, count)

    barrier = pltpu.get_barrier_semaphore()
    met = [partner, peer, other]
    met += [{"dp": away(i)} for i in range(1, count)] if direct else [near]
    for device in met:
        pl.semaphore_signal(barrier, 1, device_id=device, device_id_type=MESH)

    def remote(src, dst, send, recv, device):
        return pltpu.make_async_remote_copy(
            src, dst, send, recv, device_id=device, device_id_type=MESH
        )

    def own_copies():
        pairs_of = [(w_in.at[i], wqkv.at[pl.ds(i * kc, kq)]) for i in range(3)]
        pairs_of += [(w, home_of.at[pl.ds(0, kq)]) for w, home_of in ((w_out, wo), (c_1, w1), (c_2, w2))]
        pairs_of += [(f_1, wf1.at[0]), (f_2, wf2.at[0])]
        for e in range(ex):
            pairs_of.append((xin.at[side * ex + e], xr.at[e, side]))
        for e in range(ex):
            pairs_of.append((cin.at[side * ex + e], cot.at[e, side]))
        return [pltpu.make_async_copy(p, q, lsem.at[i]) for i, (p, q) in enumerate(pairs_of)]

    def x_copy(e):
        return remote(xin.at[(1 - side) * ex + e], xr.at[e, side], xs.at[0, e], xg.at[0, e], peer)

    def cot_copy(e):
        return remote(cin.at[(1 - side) * ex + e], cot.at[e, side], xs.at[1, e], xg.at[1, e], peer)

    def diag_copy():
        return remote(diag.at[0], diag.at[1], ts.at[0], tg.at[0], peer)

    half_kq, part_fq = kq // 2, wf1.shape[1] // 8

    def rows_at(first, n):
        return pl.ds(pl.multiple_of(first, 16), n)

    def small_ref(i):
        return (wqkv, i * kc + kq) if i < 3 else ((wo, w1, w2)[i - 3], kq)

    def big_rows(i, part):
        return rows_at((2 * ((i - W_F1[0]) % 4) + part) * part_fq, part_fq)

    def home(i, part):
        if i >= W_F1[0]:
            return (wf1, wf2)[(i - W_F1[0]) // 4].at[1, big_rows(i, part)]
        ref, first = small_ref(i)
        return ref.at[rows_at(first + part * half_kq, half_kq)]

    def w_copies(i):
        if i >= W_F1[0]:
            src = (f_1, f_2)[(i - W_F1[0]) // 4].at[big_rows(i, parity)]
            return [remote(src, home(i, parity), ys.at[i, 0], yg.at[i, 0], peer)]
        src = w_in.at[i] if i < 3 else (w_out, c_1, c_2)[i - 3]
        ref, first = small_ref(i)
        long, short = DK, half_kq - DK
        froms = (jnp.where(parity == 0, kq - DK, short), jnp.where(parity == 0, 0, DK + short))
        out = []
        for j, (at, n, skip) in enumerate(((froms[0], long, 0), (froms[1], short, long))):
            dst = ref.at[rows_at(first + parity * half_kq + skip, n)]
            out.append(remote(src.at[rows_at(at, n)], dst, ys.at[i, j], yg.at[i, j], peer))
        return out

    def w_start(order):
        for i in order:
            for cp in w_copies(i):
                cp.start()

    def w_pass(i):
        return remote(home(i, parity), home(i, parity), zps.at[i], zpg.at[i], near)

    def w_on(i):
        for cp in w_copies(i):
            cp.wait_recv()
        w_pass(i).start()

    def w_done(i):
        w_pass(i).wait()

    copies = own_copies()
    for cp in copies:
        cp.start()
    pl.semaphore_wait(barrier, len(met))
    x_copy(0).start()
    w_start((W_Q, W_K, W_V))
    values = nn(table_ref[...], hot_ref[pipe])
    at_m = lax.broadcasted_iota(jnp.int32, (1, 2 * seq), 1)
    hidden = jnp.logical_and(jnp.logical_and(at_m > 0, at_m < seq), pipe == 1)
    diag[0, 0:own_heads] = jnp.where(hidden, MASKED, values)
    diag[0, own_heads:] = jnp.zeros((8 - own_heads, 2 * seq), f32)
    diag_copy().start()
    w_start((W_O,))

    @pl.when(pipe == 0)
    def _():
        w_start((*W_F1, *W_F2, W_C1, W_C2))

    for e in range(1, ex):
        x_copy(e).start()

    @pl.when(pipe == 1)
    def _():
        w_start((W_C1, W_C2, *W_F2, *W_F1))

    for e in range(ex):
        cot_copy(e).start()
    small[...] = jnp.zeros_like(small)
    for cp in copies:
        cp.wait()
    diag_copy().wait()
    local_order = [(0, h) for h in range(own_heads)] + [(1, (h + 2) % 3) for h in range(own_heads)]
    for h, (from_side, at) in enumerate(local_order):
        wide = jnp.broadcast_to(diag[from_side, at : at + 1, :], (seq, 2 * seq))
        bias[h] = pltpu.roll(wide, 0, 1, stride=1, stride_axis=0)[:, :seq].astype(bf16)
    for i in (W_Q, W_K, W_V, W_O):
        w_on(i)
    for i in (W_Q, W_K, W_V):
        w_done(i)
    wqkv[0:kc] = wqkv[0:kc] * jnp.asarray(0.125, bf16)

    lane = lax.broadcasted_iota(jnp.int32, (1, PAIR), 1)
    half_f = [jnp.where(lane // DK == hh, 1.0, 0.0) for hh in range(2)]
    half_b = [m.astype(bf16) for m in half_f]
    key_at = lax.broadcasted_iota(jnp.int32, (1, seq), 1)

    def key_mask(length):
        return jnp.where(key_at < length, 0.0, MASKED)

    def gather_copy(kind, buf, e):
        return remote(
            buf.at[e, :, core], buf.at[e, :, core], gs.at[kind, e], gr.at[kind, e], partner
        )

    def gather_start(kind, buf, e, value):
        buf[e, :, core] = value.reshape(2, tb, width)
        gather_copy(kind, buf, e).start()

    def gather_use(kind, buf, e, fn):
        def body(i, _):
            ch = lax.rem(core + i, 2)

            @pl.when(i == 1)
            def _():
                gather_copy(kind, buf, e).wait()

            fn(buf[e, :, ch].reshape(rows, width), ch)
            return 0

        lax.fori_loop(0, 2, body, 0)

    def scatter_copy(kind, e, slot):
        return remote(rss.at[slot], rsr.at[slot], ss.at[kind, e], sr.at[kind, e], partner)

    def scatter_send(kind, e, slot, value):
        rss[slot] = value.astype(bf16)
        scatter_copy(kind, e, slot).start()

    def scatter_start(kind, e, slot, fn):
        def body(i, _):
            ch = lax.rem(core + 1 + i, 2)
            rsa[...] = fn(ch)

            @pl.when(i == 0)
            def _():
                scatter_send(kind, e, slot, rsa[...])

            return 0

        lax.fori_loop(0, 2, body, 0)

    def scatter_end(kind, e, slot):
        scatter_copy(kind, e, slot).wait()
        return rsr[slot].astype(f32)

    def scatter(kind, e, slot, fn):
        scatter_start(kind, e, slot, fn)
        return scatter_end(kind, e, slot) + rsa[...]

    def norm(v, row):
        inv = lax.rsqrt(jnp.mean(v * v, axis=-1, keepdims=True) + EPS)
        return (v * inv * gain_ref[row]).astype(bf16)

    def norm_back(v, row, grad):
        inv = lax.rsqrt(jnp.mean(v * v, axis=-1, keepdims=True) + EPS)
        unit = v * inv
        small[pl.ds(row, 1), 0:width] += jnp.sum(grad * unit, axis=0, keepdims=True)
        gg = grad * gain_ref[row]
        return inv * (gg - unit * jnp.mean(gg * unit, axis=-1, keepdims=True))

    def attend(ready, load_q, load_k, load_v, length, use_bias, store_ctx, lse_ref):
        mask = key_mask(length)

        def body(p, _):
            ready(p)
            k, v = load_k(p), load_v(p)
            for yb in range(2):
                q = load_q(yb, p)
                total = scale = None
                lse_t = lse_ref[yb]
                for hh in range(2):
                    h = 2 * p + hh
                    s = nt(q * half_b[hh], k) + mask
                    if use_bias:
                        s = s + bias[h, pl.ds(yb * rows, rows), :].astype(f32)
                    top = jnp.max(s, axis=-1, keepdims=True)
                    w = jnp.exp(s - top)
                    den = jnp.sum(w, axis=-1, keepdims=True)
                    part = nn(w.astype(bf16), v * half_b[hh])
                    total = part if total is None else total + part
                    inv = (1.0 / den) * half_f[hh]
                    scale = inv if scale is None else scale + inv
                    lse_t = jnp.where(lane == h, top + jnp.log(den), lse_t)
                store_ctx(yb, p, (total * scale).astype(bf16))
                lse_ref[yb] = lse_t
            return 0

        lax.fori_loop(0, pairs, body, 0)

    def attend_back(
        load_q, load_k, load_v, load_do, load_o, lse_ref, length, dsacc, store_dq, store_dk, store_dv
    ):
        mask = key_mask(length)

        def body(p, _):
            k, v = load_k(p), load_v(p)
            dk = dv = None
            for yb in range(2):
                q, do = load_q(yb, p), load_do(yb, p)
                both = do.astype(f32) * load_o(yb, p).astype(f32)
                lse_t = lse_ref[yb]
                dq = None
                for hh in range(2):
                    h = 2 * p + hh
                    qm, dom = q * half_b[hh], do * half_b[hh]
                    lse_c = jnp.sum(jnp.where(lane == h, lse_t, 0.0), axis=-1, keepdims=True)
                    delta = jnp.sum(both * half_f[hh], axis=-1, keepdims=True)
                    s = nt(qm, k) + mask
                    if dsacc is not None:
                        s = s + bias[h, pl.ds(yb * rows, rows), :].astype(f32)
                    w = jnp.exp(s - lse_c)
                    ds = w * (nt(dom, v) - delta)
                    wb, db = w.astype(bf16), ds.astype(bf16)
                    if dsacc is not None:
                        at = pl.ds(yb * rows, rows)
                        dsacc[h, at, :] = (dsacc[h, at, :].astype(f32) + ds).astype(bf16)
                    dvp, dkp, dqp = tn(wb, dom), tn(db, qm), nn(db, k * half_b[hh])
                    dv = dvp if dv is None else dv + dvp
                    dk = dkp if dk is None else dk + dkp
                    dq = dqp if dq is None else dq + dqp
                store_dq(yb, p, dq.astype(bf16))
            store_dk(p, dk.astype(bf16))
            store_dv(p, dv.astype(bf16))
            return 0

        lax.fori_loop(0, pairs, body, 0)

    def block_of(ref, *at):
        def lanes_at(first, p):
            return pl.ds(pl.multiple_of(first + p * PAIR, PAIR), PAIR)

        def load_rows(first=0):
            return lambda yb, p: ref[(*at, yb, slice(None), slice(None), lanes_at(first, p))].reshape(rows, PAIR)

        def load_all(first=0):
            return lambda p: ref[(*at, slice(None), slice(None), slice(None), lanes_at(first, p))].reshape(seq, PAIR)

        def store_rows(first=0):
            def store(yb, p, value):
                ref[(*at, yb, slice(None), slice(None), lanes_at(first, p))] = value.reshape(2, tb, PAIR)

            return store

        def store_all(first=0):
            def store(p, value):
                ref[(*at, slice(None), slice(None), slice(None), lanes_at(first, p))] = value.reshape(2, 2, tb, PAIR)

            return store

        return load_rows, load_all, store_rows, store_all

    def pair_of(ref, e, i):
        def load(p):
            return ref[e, p, i].reshape(seq, PAIR)

        def store(p, value):
            ref[e, p, i] = value.reshape(2, 2, tb, PAIR)

        return load, store

    def in_rows(e):
        return xr[e].reshape(rows, width).astype(f32)

    def cot_rows(e):
        return cot[e].reshape(rows, width)

    def half_rows(ref, e, ch, count):
        return ref[e, :, ch].reshape(rows, count)

    def self_forward(e, slot, length, middle=None):
        x_copy(e).wait()
        gather_start(G_IN, fin, e, norm(in_rows(e), 0))

        def project(a, ch):
            qkv[e, :, ch] = nt(a, wqkv[...]).astype(bf16).reshape(2, tb, 3 * kc)

        gather_use(G_IN, fin, e, project)
        lr, la, _, _ = block_of(qkv, e)
        _, _, store_ctx, _ = block_of(ctx, e)

        def ready(p):
            pass

        attend(ready, lr(), la(kc), la(2 * kc), length, True, store_ctx(), lse.at[e])

        @pl.when(e == 0)
        def _():
            w_done(W_O)

        if middle is not None:
            middle()

        h1[e] = in_rows(e) + scatter(
            S_ATT, e, slot, lambda ch: nn(half_rows(ctx, e, ch, kc), wo[...])
        )

    def ffn_expand(e, src, act, dg, has_grad):
        gather_start(G_FFN, ffnf, e, norm(src[e], 2))

        def expand(a, ch):
            for i in range(2):
                pre = nn(a, wf1[i])
                sq = pre * pre
                th = jnp.tanh(0.7978845608028654 * pre * (1.0 + 0.044715 * sq))
                gate = 0.5 + 0.5 * th
                slope = gate + (0.5 * 0.7978845608028654) * pre * (1.0 - th * th) * (
                    1.0 + (3 * 0.044715) * sq
                )
                lanes = pl.ds(i * fq, fq)
                act[e, :, ch, :, lanes] = (pre * gate).astype(bf16).reshape(2, tb, fq)
                if has_grad:
                    slope = slope * dg[e, :, ch, :, lanes].reshape(rows, fq).astype(f32)
                dg[e, :, ch, :, lanes] = slope.astype(bf16).reshape(2, tb, fq)

        gather_use(G_FFN, ffnf, e, expand)

    def ffn_out_part(e, act):
        return lambda ch: nn(half_rows(act, e, ch, fc), wf2[...].reshape(fc, width))

    def ffn_in_part(e, dg):
        def part(ch):
            both = half_rows(dg, e, ch, fc)
            return nt(both[:, :fq], wf1[0]) + nt(both[:, fq:], wf1[1])

        return part

    def ffn_contract(e, dg, has_slope):
        def contract(a, ch):
            for i in range(2):
                lanes = pl.ds(i * fq, fq)
                dact = nt(a, wf2[i])
                if has_slope:
                    dact = dact * dg[e, :, ch, :, lanes].reshape(rows, fq).astype(f32)
                dg[e, :, ch, :, lanes] = dact.astype(bf16).reshape(2, tb, fq)

        gather_use(G_DFFN, fffn, e, contract)

    def context_grad(kind, buf, e, w):
        def project(a, ch):
            dctx[0, :, ch] = nt(a, w[...]).astype(bf16).reshape(2, tb, kc)

        gather_use(kind, buf, e, project)

    def self_back(e, slot, length, dsacc, between=None):
        gather_start(G_DATT, fatt, e, r2[e].astype(bf16))
        context_grad(G_DATT, fatt, e, wo)
        if between is not None:
            between()
        lr, la, sr_, sa_ = block_of(qkv, e)
        ldo = block_of(dctx, 0)[0]
        lo = block_of(ctx, e)[0]
        attend_back(
            lr(), la(kc), la(2 * kc), ldo(), lo(), lse.at[e], length, dsacc,
            sr_(), sa_(kc), sa_(2 * kc),
        )
        dn = scatter(S_DIN, e, slot, lambda ch: nn(half_rows(qkv, e, ch, 3 * kc), wqkv[...]))
        hand_out(1, e, (r2[e] + norm_back(in_rows(e), 0, dn)).astype(bf16), e == ex - 1)

    def out_copies(kind, e):
        at, out = side * ex + e, (sec_out, ing_out)[kind]
        return (
            pltpu.make_async_copy(out_rows.at[e, side], out.at[at], lsem.at[8 + kind * ex + e]),
            remote(out_rows.at[e, 1 - side], out.at[at], os.at[kind, e], og.at[kind, e], peer),
        )

    def hand_out(kind, e, value, later=False):
        if kind == 1:
            for cp in out_copies(0, e):
                cp.wait()
        out_rows[e] = value.reshape(2, tb, width)

        def start():
            for cp in out_copies(kind, e):
                cp.start()

        pl.when(jnp.logical_not(later))(start)

    def pass_copy(e, p):
        return remote(kvs.at[e, p], kvr.at[e, p], ps.at[e, p], pr.at[e, p], other)

    def y_copy(u):
        return remote(ysend.at[u], yrecv.at[u], us.at[u], ug.at[u], peer)

    def all_rows(ref, lanes):
        n = lanes.size
        return ref[:, :, :, :, lanes].reshape(ex * seq, n)

    half = width // 2

    def lanes_of(r):
        return pl.ds(pl.multiple_of(r * half, PAIR), half)

    def stage_copy(gst, r, i, dst, u):
        return pltpu.make_async_copy(
            gst.at[r, :, pl.ds(i * kc, kc)], dst.at[u, lanes_of(r)], lsem.at[2 * r + i]
        )

    def drain(gst, r):
        for i in range(2):
            stage_copy(gst, r, i, gown, 0).wait()

    def ffn_grads(u, src, feed_ref, gst, pending):
        def to(dst, first, wait, sent):
            def body(r, _):
                if wait:
                    drain(gst, r)
                if sent:

                    @pl.when(r == 1)
                    def _():
                        for i in range(2):
                            y_copy(u + i).start()

                rhs = all_rows(feed_ref, pl.ds(first, fq))
                gst[r] = tn(all_rows(src, lanes_of(r)), rhs).astype(bf16)
                for i in range(2):
                    stage_copy(gst, r, i, dst, u + i).start()
                return 0

            lax.fori_loop(0, 2, body, 0)

        to(ysend, fq, pending, False)
        to(gown, 0, True, True)

    def pair_grads(u, lhs_a, load_a, lhs_b, load_b, scale, gst, pending):
        def body(r, _):
            if pending:
                drain(gst, r)
            a = tn(all_rows(lhs_a, lanes_of(r)), load_a())
            if scale is not None:
                a = a * scale
            b = tn(all_rows(lhs_b, lanes_of(r)), load_b())
            low = lane < DK
            a1, b1 = a[:, PAIR : 2 * PAIR], b[:, PAIR : 2 * PAIR]
            mix_own = jnp.where(low, a1, pltpu.roll(b1, DK, 1))
            mix_peer = jnp.where(low, pltpu.roll(a1, DK, 1), b1)
            for j, part in enumerate(
                (a[:, :PAIR], mix_own, b[:, :PAIR], a[:, 2 * PAIR :], mix_peer, b[:, 2 * PAIR :])
            ):
                gst[r, :, j * PAIR : (j + 1) * PAIR] = part.astype(bf16)
            for i, dst in enumerate((gown, ysend)):
                stage_copy(gst, r, i, dst, u).start()
            return 0

        lax.fori_loop(0, 2, body, 0)
        for r in range(2):
            drain(gst, r)
        y_copy(u).start()

    def z_copy(u, step):
        block = width // count
        at = away(step)
        return remote(
            zs.at[u, pl.ds(pl.multiple_of(at * block, 16), block)], zr.at[u, step - 1],
            vs.at[u, step - 1], vg.at[u, step - 1], {"dp": at},
        )

    def pump(u, gst):
        y_copy(u).wait_recv()
        loads, stores = [], []
        for r in range(2):
            own, came = gst.at[r, :, pl.ds(0, kc)], gst.at[r, :, pl.ds(kc, kc)]
            loads.append(pltpu.make_async_copy(gown.at[u, lanes_of(r)], own, lsem.at[4 + r]))
            loads.append(pltpu.make_async_copy(yrecv.at[u, lanes_of(r)], came, lsem.at[6 + r]))
            stores.append(pltpu.make_async_copy(own, zs.at[u, lanes_of(r)], lsem.at[4 + r]))
        for cp in loads:
            cp.start()
        for r in range(2):
            for cp in loads[2 * r : 2 * r + 2]:
                cp.wait()
            gst[r, :, 0:kc] = (
                gst[r, :, 0:kc].astype(f32) + gst[r, :, kc : 2 * kc].astype(f32)
            ).astype(bf16)
            stores[r].start()
        for cp in stores:
            cp.wait()
        if direct:
            for step in range(1, count):
                z_copy(u, step).start()

    def finish(u, va, vf):
        block = width // count
        for step in range(1, count):
            z_copy(u, step).wait()
        mine = pl.ds(pl.multiple_of(data * block, 16), block)
        cps = [pltpu.make_async_copy(zs.at[u, mine], va.at[pl.ds(0, block)], lsem.at[0])]
        for step in range(1, count):
            cps.append(
                pltpu.make_async_copy(
                    zr.at[u, step - 1], va.at[pl.ds(step * block, block)], lsem.at[step]
                )
            )
        for cp in cps:
            cp.start()
        for cp in cps:
            cp.wait()
        total = va[0:block].astype(f32)
        for step in range(1, count):
            total = total + va[step * block : (step + 1) * block].astype(f32)
        vf[...] = total
        cp = pltpu.make_async_copy(vf, fin_out.at[u], lsem.at[0])
        cp.start()
        cp.wait()

    def small_near():
        first = remote(small.at[pl.ds(0, 8)], small_c, ms.at[0], mg.at[0], partner)
        first.start()
        first.wait()
        small[0:8] += small_c[...]
        small_peer().start()

    def small_peer():
        return remote(small, small_y, ms.at[1], mg.at[1], peer)

    def small_far():
        return [
            remote(small, small_z.at[i - 1], ms.at[1 + i], mg.at[1 + i], {"dp": away(i)})
            for i in range(1, count)
        ]

    def small_middle():
        small_peer().wait()
        small[0:8] += small_y[0:8]
        for h in range(own_heads):
            at = 8 + own_heads + (h + 1) % 3
            small[8 + h : 9 + h] += small_y[at : at + 1]
        if direct:
            for cp in small_far():
                cp.start()

    def small_end():
        total = small[...]
        if direct:
            for cp in small_far():
                cp.wait()
            for i in range(1, count):
                total = total + small_z[i - 1]
        small_out[...] = total

    def bias_grads(dsacc):
        at_r = lax.broadcasted_iota(jnp.int32, (seq, seq), 0)
        at_c = lax.broadcasted_iota(jnp.int32, (seq, seq), 1)
        flip = jnp.where(at_r + at_c == seq - 1, 1.0, 0.0).astype(bf16)

        def body(h, _):
            reverse = nn(dsacc[h], flip)
            wide = jnp.concatenate([reverse, jnp.zeros((seq, seq), f32)], axis=1)
            wide = pltpu.roll(wide, 0, 1, stride=1, stride_axis=0)
            small[pl.ds(8 + h, 1), :] = jnp.sum(wide, axis=0, keepdims=True)
            return 0

        lax.fori_loop(0, heads, body, 0)

    def loop(fn):
        def body(e, _):
            fn(e)
            return 0

        lax.fori_loop(0, ex, body, 0)

    def last_grads(dsacc, gst, between, small_first):
        def small_now():
            bias_grads(dsacc)
            small_near()

        lanes = [pl.ds(i * kc, kc) for i in range(3)]
        if small_first:
            small_now()
            between()
        pair_grads(
            5, fin, lambda: all_rows(qkv, lanes[0]), fin, lambda: all_rows(qkv, lanes[1]),
            0.125, gst, False,
        )
        pair_grads(
            6, fin, lambda: all_rows(qkv, lanes[2]), fatt, lambda: all_rows(ctx, lanes[0]),
            None, gst, False,
        )
        if not small_first:
            between()
            small_now()
        for cp in out_copies(1, ex - 1):
            cp.start()

    def collect(order, done, gst, small_first):
        def run(va, vf):
            n = len(order)
            ended = 0
            for k in range(done, n):
                if direct:
                    while ended <= k - 3:
                        finish(order[ended], va, vf)
                        ended += 1
                if k == n - 1 and small_first:
                    small_middle()
                pump(order[k], gst)
            if not small_first:
                small_middle()
            if direct:
                while ended < n:
                    finish(order[ended], va, vf)
                    ended += 1
            small_end()
            for u in order:
                y_copy(u).wait_send()
            for e in range(ex):
                for cp in out_copies(1, e):
                    cp.wait()

        V = pltpu.VMEM
        pl.run_scoped(run, V((width, kc), bf16), V((width // count, kc), f32))

    def begun():
        for i in range(WEIGHTS):
            for cp in w_copies(i):
                cp.wait_send()
        for e in range(ex):
            cot_copy(e).wait_send()

    V = pltpu.VMEM
    feed = V((ex, 2, 2, tb, fc), bf16)
    grad_stage = V((2, half, 2 * kc), bf16)
    score_sums = V((heads, seq, seq), bf16)
    last = ex - 1

    def pass_all(e, fn):
        for p in range(pairs):
            fn(pass_copy(e, p))

    def wide(ref, e, i, ch):
        return jnp.concatenate([ref[e, p, i, :, ch].reshape(rows, PAIR) for p in range(pairs)], 1)

    @pl.when(pipe == 0)
    def _():
        def own_length(e):
            return len_ref[0, side * ex + e]

        def keys(i):
            return lambda: jnp.concatenate(
                [kvr[:, p, i].reshape(ex * seq, PAIR) for p in range(pairs)], 1
            )

        def run(act, dg, dsacc, gst):
            def ahead(e):
                def middle():
                    pl.when(e == 0)(lambda: w_on(W_F1[0]))

                self_forward(e, 0, own_length(e), middle)

                @pl.when(e == 0)
                def _():
                    for i in (*W_F1[1:], *W_F2[:2]):
                        w_on(i)
                    for i in W_F1:
                        w_done(i)

                ffn_expand(e, h1, act, dg, False)

                @pl.when(e == 0)
                def _():
                    for i in W_F2[2:]:
                        w_on(i)
                    for i in W_F2:
                        w_done(i)
                    for i in (W_C1, W_C2):
                        w_on(i)

                r2[e] = h1[e] + scatter(S_FFN, e, 1, ffn_out_part(e, act))
                memory = norm(r2[e], 1)
                gather_start(G_MID, mid, e, memory)
                hand_out(0, e, memory)

                @pl.when(e == 0)
                def _():
                    for i in (W_C1, W_C2):
                        w_done(i)

                def project(a, ch):
                    for i, w in enumerate((w1, w2)):
                        out = nt(a, w[...]).astype(bf16)
                        for p in range(pairs):
                            kvs[e, p, i, :, ch] = out[:, p * PAIR : (p + 1) * PAIR].reshape(
                                2, tb, PAIR
                            )

                gather_use(G_MID, mid, e, project)
                pass_all(e, lambda cp: cp.start())

            def back(e):
                pass_all(e, lambda cp: cp.wait())
                cot_copy(e).wait_recv()

                def partial_sum(ch):
                    return nn(wide(kvr, e, 0, ch), w1[...]) + nn(wide(kvr, e, 1, ch), w2[...])

                scatter_start(S_DMEM, e, 1, partial_sum)

                @pl.when(e == last)
                def _():
                    pair_grads(4, mid, keys(0), mid, keys(1), None, gst, False)

                dmem = cot_rows(e).astype(f32) + (scatter_end(S_DMEM, e, 1) + rsa[...])
                r2[e] = norm_back(r2[e], 1, dmem)
                gather_start(G_DFFN, fffn, e, r2[e].astype(bf16))
                ffn_contract(e, dg, True)
                scatter_start(S_DFFN, e, 0, ffn_in_part(e, dg))

                @pl.when(e == last)
                def _():
                    ffn_grads(2, fffn, act, gst, False)

                dn = scatter_end(S_DFFN, e, 0) + rsa[...]
                r2[e] += norm_back(h1[e], 2, dn)

                @pl.when(e == last)
                def _():
                    for r in range(2):
                        drain(gst, r)
                    pump(4, gst)
                    ffn_grads(0, ffnf, dg, gst, False)
                    for r in range(2):
                        drain(gst, r)

                self_back(
                    e, 0, own_length(e), dsacc, lambda: pl.when(e == last)(lambda: pump(2, gst))
                )

            loop(ahead)
            dsacc[...] = jnp.zeros_like(dsacc)
            begun()
            loop(back)

        def outer(dsacc, gst):
            pl.run_scoped(lambda act, dg: run(act, dg, dsacc, gst), feed, feed)
            pump(3, gst)
            last_grads(dsacc, gst, lambda: pump(0, gst), True)
            collect((4, 2, 3, 0, 1, 5, 6), 4, gst, True)

        pl.run_scoped(outer, score_sums, grad_stage)

    @pl.when(pipe == 1)
    def _():
        def own_length(e):
            return len_ref[1, side * ex + e]

        def run(act, dg, cq, cctx, clse, gst):
            def first(e):
                self_forward(e, lax.rem(e, 2), own_length(e))
                gather_start(G_MID, mid, e, norm(h1[e], 1))

            def second(e):
                def project(a, ch):
                    cq[e, :, ch] = nt(a, w1[...]).astype(bf16).reshape(2, tb, kc)

                gather_use(G_MID, mid, e, project)

            def third(e):
                cot_copy(e).wait_recv()
                gather_start(G_DFFN, fffn, e, cot_rows(e))

            def there_and_back(e):
                lq, _, sq, _ = block_of(cq, e)
                (lk, _), (lv, _) = pair_of(kvr, e, 0), pair_of(kvr, e, 1)
                lc, _, sc, _ = block_of(cctx, e)
                source_length = len_ref[0, side * ex + e]
                attend(
                    lambda p: pass_copy(e, p).wait_recv(), lq(), lk, lv, source_length, False,
                    sc(), clse,
                )
                r2[e] = h1[e] + scatter(
                    S_MID, e, 1, lambda ch: nn(half_rows(cctx, e, ch, kc), w2[...])
                )
                ffn_expand(e, r2, act, dg, True)
                scatter_start(S_DFFN, e, 0, ffn_in_part(e, dg))
                scatter_send(S_FFN, e, 2, ffn_out_part(e, act)(1 - core))
                dn = scatter_end(S_DFFN, e, 0) + rsa[...]
                h2 = r2[e]
                grad = cot_rows(e).astype(f32) + norm_back(h2, 2, dn)
                rsa[...] = h2
                r2[e] = grad
                gather_start(G_DMID, fmid, e, grad.astype(bf16))
                out = rsa[...] + ffn_out_part(e, act)(core)
                hand_out(0, e, (out + scatter_end(S_FFN, e, 2)).astype(bf16))
                context_grad(G_DMID, fmid, e, w2)
                ldo = block_of(dctx, 0)[0]
                sk, sv = pair_of(kvs, e, 0)[1], pair_of(kvs, e, 1)[1]

                def store_values(p, value):
                    sv(p, value)
                    pass_copy(e, p).start()

                attend_back(
                    lq(), lk, lv, ldo(), lc(), clse, source_length, None, sq(), sk, store_values
                )


            def finish_cross(e):
                dn = scatter(S_DMID, e, lax.rem(e, 2), lambda ch: nn(half_rows(cq, e, ch, kc), w1[...]))
                r2[e] += norm_back(h1[e], 1, dn)

            loop(first)
            for i in (W_C1, W_C2, *W_F2[:2]):
                w_on(i)
            for i in (W_C1, W_C2):
                w_done(i)
            w1[...] = w1[...] * jnp.asarray(0.125, bf16)
            loop(second)
            for i in (*W_F2[2:], *W_F1):
                w_on(i)
            loop(third)
            for i in W_F2:
                w_done(i)
            loop(lambda e: ffn_contract(e, dg, False))
            for i in W_F1:
                w_done(i)
            begun()
            loop(there_and_back)
            ffn_grads(2, fffn, act, gst, False)
            ffn_grads(0, ffnf, dg, gst, True)
            lanes = pl.ds(0, kc)
            pair_grads(
                4, mid, lambda: all_rows(cq, lanes), fmid, lambda: all_rows(cctx, lanes),
                0.125, gst, True,
            )
            pump(2, gst)
            loop(finish_cross)

        pl.run_scoped(
            run, feed, feed, V((ex, 2, 2, tb, kc), bf16), V((ex, 2, 2, tb, kc), bf16),
            V((2, rows, PAIR), f32), grad_stage,
        )

        def outer(dsacc, gst):
            dsacc[...] = jnp.zeros_like(dsacc)

            def body(e):
                def between():
                    pl.when(e == 0)(lambda: pump(3, gst))
                    pl.when(e == last)(lambda: pump(4, gst))

                self_back(e, 1 - lax.rem(e, 2), own_length(e), dsacc, between)
                pl.when(e < last)(lambda: pump(e, gst))

            loop(body)
            loop(lambda e: pass_all(e, lambda cp: cp.wait_send()))
            last_grads(dsacc, gst, lambda: None, False)
            collect((2, 3, 0, 1, 4, 5, 6), 5, gst, False)

        pl.run_scoped(outer, score_sums, grad_stage)


def run_sections(x, cot, w_in, w_out, c_1, c_2, f_1, f_2, gains, lens, table, hot, direct):
    batch, tb, width = x.shape
    ex = batch // 2
    rows, seq = 2 * tb, 4 * tb
    kq, fq = w_out.shape[0], f_1.shape[1]
    kc, fc = 2 * kq, 2 * fq
    heads = kc // DK
    count = lax.axis_size("dp")
    vmem = pl.BlockSpec(memory_space=pltpu.VMEM)
    hbm = pl.BlockSpec(memory_space=pl.ANY)
    smem = pl.BlockSpec(memory_space=pltpu.SMEM)
    full = (ex, 2, 2, tb)
    units = (7, width, kc)
    V = pltpu.VMEM
    D = pltpu.SemaphoreType.DMA
    S = jax.ShapeDtypeStruct
    scratch = [
        V((3 * kc, width), bf16), V((kc, width), bf16), V((kc, width), bf16), V((kc, width), bf16),
        V((2, width, fq), bf16), V((2, fq, width), bf16), V((heads, seq, seq), bf16),
        V((ex, 2, tb, width), bf16), V((ex, 2, tb, width), bf16),
        V((ex, 2, tb, width), bf16),
        V((*full, width), bf16),
        V((*full, 3 * kc), bf16),
        V((*full, kc), bf16),
        V((ex, 2, rows, PAIR), f32),
        V((ex, rows, width), f32),
        V((*full, width), bf16),
        V((*full, width), bf16),
        V((ex, kc // PAIR, 2, 2, 2, tb, PAIR), bf16),
        V((ex, kc // PAIR, 2, 2, 2, tb, PAIR), bf16),
        V((ex, rows, width), f32),
        V((*full, width), bf16),
        V((*full, width), bf16),
        V((1, 2, 2, tb, kc), bf16),
        V((rows, width), f32),
        V((3, rows, width), bf16),
        V((3, rows, width), bf16),
        V((2, 8, 2 * seq), f32),
        V((16, 2 * seq), f32), V((8, 2 * seq), f32), V((16, 2 * seq), f32),
        V((max(1, count - 1) if direct else 1, 16, 2 * seq), f32),
        D((8 + 2 * ex,)),
        D((2, ex)), D((2, ex)), D((1,)), D((1,)), D((WEIGHTS, 2)), D((WEIGHTS, 2)), D((WEIGHTS,)), D((WEIGHTS,)),
        D((6, ex)), D((6, ex)), D((7, ex)), D((7, ex)), D((ex, kc // PAIR)), D((ex, kc // PAIR)),
        D((2, ex)), D((2, ex)), D((7,)), D((7,)), D((7, 3)), D((7, 3)), D((5,)), D((5,)),
    ]
    slots = count - 1 if direct else 1
    return pl.pallas_call(
        partial(section_kernel, direct=direct),
        out_shape=(
            S((batch, tb, width), bf16),
            S((batch, tb, width), bf16),
            S(units, bf16),
            S((7, slots, width // count if direct else 16, kc), bf16),
            S((7, width // count if direct else 8, kc), f32),
            S((16, 2 * seq), f32),
            S(units, bf16),
            S(units, bf16),
            S(units, bf16),
        ),
        in_specs=[hbm] * 8 + [vmem, smem, vmem, vmem],
        out_specs=(hbm, hbm, hbm, hbm, hbm, vmem, hbm, hbm, hbm),
        scratch_shapes=scratch,
        compiler_params=pltpu.CompilerParams(
            collective_id=0, has_side_effects=True, vmem_limit_bytes=64 * 2**20 - 65536
        ),
        name="sections",
    )(x, cot, w_in, w_out, c_1, c_2, f_1, f_2, gains, lens, table, hot)


def ends_kernel(
    sec, ing, fin_hbm, small, hot_ref,
    o_sec, o_ing, o_in, o_out, o_c1, o_c2, o_f1, o_f2, o_bias, o_gain,
    low_rows, high_rows, out_rows, fin, lsem, ssem,
):
    batch = ing.shape[0]
    whole_in = pltpu.make_async_copy(sec, out_rows, lsem.at[batch])
    whole = pltpu.make_async_copy(out_rows, o_sec.at[0], lsem.at[batch])
    sums_in = pltpu.make_async_copy(fin_hbm, fin, lsem.at[batch + 1])
    loads = [pltpu.make_async_copy(ing.at[e], low_rows.at[e], lsem.at[e]) for e in range(batch)]
    stores = [
        pltpu.make_async_copy(high_rows.at[e], o_ing.at[0, e], ssem.at[e]) for e in range(batch)
    ]
    for cp in loads:
        cp.start()
    sums_in.start()
    whole_in.start()
    for e in range(batch):
        loads[e].wait()
        high_rows[e] = low_rows[e].astype(f32)
        stores[e].start()
    whole_in.wait()
    whole.start()
    sums_in.wait()

    def first(u):
        return jnp.concatenate([fin[u, :, :PAIR], fin[u, :, PAIR : PAIR + DK]], 1)

    def second(u):
        return jnp.concatenate([fin[u, :, 2 * PAIR :], fin[u, :, PAIR + DK : 2 * PAIR]], 1)

    o_in[0, 0], o_in[0, 1], o_in[0, 2] = first(5), second(5), first(6)
    o_out[0] = second(6).T
    o_c1[0], o_c2[0] = first(4), second(4)
    kc = fin.shape[2]
    for i in range(2):
        o_f1[0, :, i * kc : (i + 1) * kc] = fin[i]
        o_f2[0, :, i * kc : (i + 1) * kc] = fin[2 + i]
    sums = small[8:16, :]
    high = sums.astype(bf16)
    rest = sums - high.astype(f32)
    middle = rest.astype(bf16)
    low = (rest - middle.astype(f32)).astype(bf16)
    hot = hot_ref[lax.axis_index("pipe"), lax.axis_index("dp")]
    bias = nt(high, hot) + nt(middle, hot) + nt(low, hot)
    for h in range(o_bias.shape[0]):
        o_bias[h] = bias[h : h + 1]
    share = o_gain.shape[2]
    at = (lax.axis_index("dp") * lax.axis_size("tensor") + lax.axis_index("tensor")) * share
    moved = pltpu.roll(small[0:8, :], lax.rem(small.shape[1] - at, small.shape[1]), 1)
    for i in range(3):
        o_gain[i] = moved[i : i + 1, :share]
    whole.wait()
    for cp in stores:
        cp.wait()


def ends(sec, ing, fin, small, hot, share, heads):
    batch, tb, width = ing.shape
    _, block, kc = fin.shape
    kq = kc // 2
    S = jax.ShapeDtypeStruct
    D = pltpu.SemaphoreType.DMA
    vmem = pl.BlockSpec(memory_space=pltpu.VMEM)
    hbm = pl.BlockSpec(memory_space=pl.ANY)
    return pl.pallas_call(
        ends_kernel,
        out_shape=(
            S((1, batch, tb, width), bf16), S((1, batch, tb, width), f32),
            S((1, 3, block, kq), f32), S((1, kq, block), f32),
            S((1, block, kq), f32), S((1, block, kq), f32), S((1, block, 2 * kc), f32),
            S((1, block, 2 * kc), f32), S((heads, 1, hot.shape[2]), f32), S((3, 1, share), f32),
        ),
        in_specs=[hbm, hbm, hbm, vmem, vmem],
        out_specs=(hbm, hbm) + (vmem,) * 8,
        scratch_shapes=[
            pltpu.VMEM((batch, tb, width), bf16), pltpu.VMEM((batch, tb, width), f32),
            pltpu.VMEM((batch, tb, width), bf16), pltpu.VMEM(fin.shape, f32), D((batch + 2,)), D((batch,)),
        ],
        compiler_params=pltpu.CompilerParams(vmem_limit_bytes=64 * 2**20 - 65536),
        name="ends",
    )(sec, ing, fin, small, hot)


def local(
    section_input, lengths, norm_gain, attn_in, attn_out, cross_first, cross_second,
    ffn_in, ffn_out, rel_bias, out_grad,
):
    enc = lax.axis_index("pipe") == 0
    tb, width = section_input.shape[2:]
    seq = tb * lax.axis_size("tensor")
    kq = attn_out.shape[1]
    data = lax.axis_size("dp")
    at_data = lax.axis_index("dp")
    direct = data <= 4 and (width // data) % 16 == 0
    heads = kq // DK

    offsets = list(range(seq)) + [0] + list(range(-seq + 1, 0))
    both = [np.array(bucket_list(offsets, ways)) for ways in (True, False)]
    hot = np.stack([np.arange(NB)[:, None] == spots[None] for spots in both])
    turned = [seq - 1 - m for m in range(2 * seq)]
    hot_m = np.stack(
        [np.arange(NB)[:, None] == np.array(bucket_list(turned, ways)) for ways in (True, False)]
    )

    def across(w):
        return jnp.swapaxes(w, -1, -2)

    sec, ing, zs, _, fin, small, _, _, _ = run_sections(
        section_input[0], out_grad[0], across(attn_in[0]), attn_out[0], across(cross_first[0]),
        across(cross_second[0]), ffn_in[0], ffn_out[0], jnp.swapaxes(norm_gain, 0, 1),
        lengths.T, rel_bias[0].T, jnp.asarray(hot, bf16), direct,
    )
    share = width // (data * lax.axis_size("tensor"))
    if direct:
        by_data = jnp.asarray(hot_m.reshape(2, data, NB // data, 2 * seq), bf16)
        sec, ing, w_in, w_out, c_1, c_2, f_1, f_2, bias, gains = ends(
            sec, ing, fin, small, by_data, share, heads
        )
        return (
            sec, ing, w_in, w_out, c_1, c_2, f_1, across(f_2),
            jnp.transpose(bias, (1, 2, 0)), jnp.swapaxes(gains, 0, 1),
        )

    packed = zs.reshape(7, data, width // data, 2 * kq)
    shard = lax.psum_scatter(packed, "dp", scatter_dimension=1, tiled=False).astype(f32)
    hot_m = jnp.where(enc, jnp.asarray(hot_m[0], f32), jnp.asarray(hot_m[1], f32))
    bsum = jnp.einsum("bm,hm->bh", hot_m, small[8 : 8 + heads], precision=lax.Precision.HIGHEST)
    bias_grad = lax.psum_scatter(bsum, "dp", scatter_dimension=0, tiled=True)
    gains = lax.psum(small[:3, :width], "dp")
    at = (at_data * lax.axis_size("tensor") + lax.axis_index("tensor")) * share
    gain_grad = lax.dynamic_slice_in_dim(gains, at, share, 1)

    def first_of(u):
        return jnp.concatenate([shard[u, :, :PAIR], shard[u, :, PAIR : PAIR + DK]], 1)

    def second_of(u):
        return jnp.concatenate([shard[u, :, 2 * PAIR :], shard[u, :, PAIR + DK : 2 * PAIR]], 1)

    return (
        sec[None],
        ing[None].astype(f32),
        jnp.stack([first_of(5), second_of(5), first_of(6)])[None],
        second_of(6).T[None],
        first_of(4)[None],
        second_of(4)[None],
        jnp.concatenate([shard[0], shard[1]], 1)[None],
        jnp.concatenate([shard[2], shard[3]], 1).T[None],
        bias_grad[None],
        gain_grad[None],
    )


def solution(mesh):
    placed = (
        P("pipe", "dp", "tensor", None),
        P("dp", None),
        P("pipe", None, None),
        P("pipe", None, None, "tensor"),
        P("pipe", "tensor", None),
        P("pipe", None, "tensor"),
        P("pipe", None, "tensor"),
        P("pipe", None, "tensor"),
        P("pipe", "tensor", None),
        P("pipe", None, "tensor"),
        P("pipe", "dp", "tensor", None),
    )
    return jax.shard_map(
        local,
        mesh=mesh,
        in_specs=placed,
        out_specs=(
            P("pipe", "dp", "tensor", None),
            P("pipe", "dp", "tensor", None),
            P("pipe", None, "dp", "tensor"),
            P("pipe", "tensor", "dp"),
            P("pipe", "dp", "tensor"),
            P("pipe", "dp", "tensor"),
            P("pipe", "dp", "tensor"),
            P("pipe", "tensor", "dp"),
            P("pipe", "dp", "tensor"),
            P("pipe", None, ("dp", "tensor")),
        ),
        check_vma=False,
    )
```

profile of v0, /device:TPU:0, one launch (start us, length us, event | category | flops | bytes accessed | tf_op | source)
XLA Modules:
  0.0 316.2 jit_solution(10435232896410407795)
XLA Ops:
  0.6 308.6 %sections.1 = (bf16[6,128,768]{2,1,0:T(8,128)(2,1)}, bf16[6,128,768]{2,1,0:T(8,128)(2,1)}, bf16[7,768,384]{2,1,0:T(8,128)(2,1)}, bf16[7,3,192,384]{3,2,1,0:T(8,1...) custom-call(bf16[6,128,768]{2,1,0:T(8,128)(2,1)} %bitcast.22, ...), custom_call_target="tpu_custom_call" | custom-call | tf_op jit(solution)/shard_map/sections/pallas_call | solution.py:1017
  309.3 6.7 %ends.1 = (bf16[1,6,128,768]{3,2,1,0:T(8,128)(2,1)}, f32[1,6,128,768]{3,2,1,0:T(8,128)}, f32[1,3,192,192]{3,2,1,0:T(8,128)}, f32[1,192,192]{2,1,0:T(8,128)}, f32...) custom-call(bf16[6,128,768]{2,1,0:T(8,128)(2,1)} %get-tuple-element., ...), custom_call_target="tpu_custom_call" | custom-call | tf_op jit(solution)/shard_map/ends/pallas_call | solution.py:1105
where the time goes:
time: 321 us; the launch traced here: 316 us
  Pallas kernels  315 us (98%)
    pallas_call x1, Pallas kernels, run_sections(): pl.pallas_call(partial(section_kernel, direct=direct), out_shape=(S((batc...  309 us
    pallas_call x1, Pallas kernels, ends(): pl.pallas_call(ends_kernel, out_shape=(S((1, batch, tb, width), bf16), S(...  6.71 us

commit v1 on v0

--- a/solution.py
+++ b/solution.py
@@ -171,16 +171,15 @@
     copies = own_copies()
     for cp in copies:
         cp.start()
-    pl.semaphore_wait(barrier, len(met))
-    x_copy(0).start()
-    w_start((W_Q, W_K, W_V))
     values = nn(table_ref[...], hot_ref[pipe])
     at_m = lax.broadcasted_iota(jnp.int32, (1, 2 * seq), 1)
     hidden = jnp.logical_and(jnp.logical_and(at_m > 0, at_m < seq), pipe == 1)
     diag[0, 0:own_heads] = jnp.where(hidden, MASKED, values)
     diag[0, own_heads:] = jnp.zeros((8 - own_heads, 2 * seq), f32)
+    pl.semaphore_wait(barrier, len(met))
     diag_copy().start()
-    w_start((W_O,))
+    x_copy(0).start()
+    w_start((W_Q, W_K, W_V, W_O))
 
     @pl.when(pipe == 0)
     def _():
@@ -196,15 +195,16 @@
     for e in range(ex):
         cot_copy(e).start()
     small[...] = jnp.zeros_like(small)
-    for cp in copies:
-        cp.wait()
     diag_copy().wait()
     local_order = [(0, h) for h in range(own_heads)] + [(1, (h + 2) % 3) for h in range(own_heads)]
     for h, (from_side, at) in enumerate(local_order):
         wide = jnp.broadcast_to(diag[from_side, at : at + 1, :], (seq, 2 * seq))
         bias[h] = pltpu.roll(wide, 0, 1, stride=1, stride_axis=0)[:, :seq].astype(bf16)
-    for i in (W_Q, W_K, W_V, W_O):
+    for i in (W_Q, W_K, W_V):
         w_on(i)
+    for cp in copies:
+        cp.wait()
+    w_on(W_O)
     for i in (W_Q, W_K, W_V):
         w_done(i)
     wqkv[0:kc] = wqkv[0:kc] * jnp.asarray(0.125, bf16)

time: 321 us -> 315 us (0.981)
  Pallas kernels: 315 us -> 309 us
    pallas_call x1, Pallas kernels: 309 us -> 303 us  [run_sections(): pl.pallas_call(partial(section_kernel, direct=direct), out_shape=(S((batc...]
where the time goes in v1:
time: 315 us; the launch traced here: 310 us
  Pallas kernels  309 us (98%)
    pallas_call x1, Pallas kernels, run_sections(): pl.pallas_call(partial(section_kernel, direct=direct), out_shape=(S((batc...  303 us
    pallas_call x1, Pallas kernels, ends(): pl.pallas_call(ends_kernel, out_shape=(S((1, batch, tb, width), bf16), S(...  6.71 us

profile of v1, /device:TPU:0, one launch (start us, length us, event | category | flops | bytes accessed | tf_op | source)
XLA Modules:
  0.0 310.2 jit_solution(18157310233675383634)
XLA Ops:
  0.6 302.6 %sections.1 = (bf16[6,128,768]{2,1,0:T(8,128)(2,1)}, bf16[6,128,768]{2,1,0:T(8,128)(2,1)}, bf16[7,768,384]{2,1,0:T(8,128)(2,1)}, bf16[7,3,192,384]{3,2,1,0:T(8,1...) custom-call(bf16[6,128,768]{2,1,0:T(8,128)(2,1)} %bitcast.22, ...), custom_call_target="tpu_custom_call" | custom-call | tf_op jit(solution)/shard_map/sections/pallas_call | solution.py:1017
  303.3 6.7 %ends.1 = (bf16[1,6,128,768]{3,2,1,0:T(8,128)(2,1)}, f32[1,6,128,768]{3,2,1,0:T(8,128)}, f32[1,3,192,192]{3,2,1,0:T(8,128)}, f32[1,192,192]{2,1,0:T(8,128)}, f32...) custom-call(bf16[6,128,768]{2,1,0:T(8,128)(2,1)} %get-tuple-element., ...), custom_call_target="tpu_custom_call" | custom-call | tf_op jit(solution)/shard_map/ends/pallas_call | solution.py:1105
